TPU v7x, 512 devices: a whole 4x8x8 slice. The times are simulated.
512 devices in a mesh: row: 16 (over z_lo, x), col: 8 (over y), fiber: 4 (over z_hi, core).
Axes of the slice: x: 4, y: 8, z: 8 (z_hi: 2, z_lo: 4; z = z_hi * 4 + z_lo), core: 2. Of those that a mesh axis runs over, the one named last changes fastest.
Arguments:
- values: float32 [12288, 12288], P('row', ('col', 'fiber')), may hold values from -6 to 6
- tile_mask: int32 [96, 96], P('row', ('col', 'fiber')), may hold values from 0 to 1, as said below
- keep_mask: int32 [96, 96], P('row', ('col', 'fiber')), may hold values 0 or 1
Outputs:
- flows: float32 [12288, 12288], P('row', ('col', 'fiber'))
Inputs may be any that keep to these rules, and one draw needn't show every extreme that they name: `tile_mask`: 1 marks a tile that holds entries; every diagonal tile is 1, and tiles with low indices are denser.
All inputs are finite; a program needn't handle non-finite values. No bound on the sum of `keep_mask` on one device may be relied on, other than what follows from the above.
Results may differ from a plain program's by a relative error of at most 0.017.
Values may be sent and summed in bfloat16 or wider, within the bound.
No kernel may reach another device: no remote copies, remote signals or barrier semaphores. Data moves between devices by JAX's collectives and lax.ppermute only.
A program may use at most 64 MiB of HBM per device.

v0:
```python
import jax
import jax.numpy as jnp
from jax import lax
from jax.sharding import PartitionSpec as P


def cut_along(shard, dim, peers):
    lengths = shard.shape
    parts = shard.reshape(*lengths[:dim], peers, lengths[dim] // peers, *lengths[dim + 1 :])
    return jnp.moveaxis(parts, dim, 0)


def sum_at_owner(shard, axis, dim):
    parts = cut_along(shard, dim, lax.axis_size(axis))
    arrived = lax.all_to_all(parts, axis, split_axis=0, concat_axis=0, tiled=True)
    return arrived.astype(jnp.float32).sum(axis=0)


def sent_to_all(shard, axis):
    copies = jnp.broadcast_to(shard, (lax.axis_size(axis), *shard.shape))
    return lax.all_to_all(copies, axis, split_axis=0, concat_axis=0, tiled=True)


def taken_together(shard, axis):
    return sent_to_all(shard, axis).sum(axis=0)


def spread_tiles(mask, tile_size):
    count_rows, count_cols = mask.shape
    wide = jnp.broadcast_to(
        mask.astype(jnp.float32)[:, None, :, None], (count_rows, tile_size, count_cols, tile_size)
    )
    return wide.reshape(count_rows * tile_size, count_cols * tile_size)


def local(values, tile_mask, keep_mask):
    n_row = lax.axis_size("row")
    n_fib = lax.axis_size("fiber")
    tile_size = values.shape[1] // tile_mask.shape[1]
    weighted = (values * spread_tiles(tile_mask, tile_size)).astype(jnp.bfloat16)
    rows_dev, unit_width = weighted.shape
    sub_width = unit_width // n_fib
    unit_count = rows_dev // unit_width
    left_stack = weighted.reshape(rows_dev, n_fib, sub_width)
    right_stack = weighted.reshape(unit_count, n_fib, sub_width, unit_width)
    left_recv, right_recv = (
        lax.all_to_all(left_stack, "fiber", split_axis=1, concat_axis=1, tiled=True),
        lax.all_to_all(right_stack, "fiber", split_axis=1, concat_axis=1, tiled=True),
    )
    left_local = left_recv.reshape(rows_dev, unit_width)
    right_local = jnp.transpose(right_recv, (0, 2, 1, 3)).reshape(
        unit_count * sub_width, n_fib * unit_width
    )
    left_all = lax.all_gather(left_local, "col", axis=1, tiled=True)
    partial_product = jnp.dot(
        left_all,
        lax.all_gather(right_local, "row", axis=0, tiled=True),
        preferred_element_type=jnp.float32,
    )
    expanded = sum_at_owner(partial_product.astype(jnp.bfloat16), "fiber", 1)
    squared = expanded * expanded
    col_total = taken_together(jnp.sum(squared, axis=0), "row")
    col_scale = col_total / (rows_dev * n_row) + 1e-06
    return spread_tiles(keep_mask, tile_size) * squared / col_scale[None, :]


def solution(mesh):
    return jax.shard_map(
        local,
        mesh=mesh,
        in_specs=(
            P("row", ("col", "fiber")),
            P("row", ("col", "fiber")),
            P("row", ("col", "fiber")),
        ),
        out_specs=P("row", ("col", "fiber")),
        check_vma=False,
    )
```

profile of v0, /device:TPU:8, one launch (start us, length us, event | category | flops | bytes accessed | tf_op | source)
XLA Modules:
  0.0 311.7 jit_solution(8198016643156649648)
XLA Ops:
  6.5 0.0 all-gather.3.cloned.1.call-start
  6.5 0.7 convert_element_type.16
  7.2 1.6 copy.27
  8.9 0.2 broadcast_in_dim.7
  9.0 0.4 fusion
  9.4 30.0 %all_to_all.21 = bf16[768,4,96]{0,2,1:T(8,128)(2,1)} all-to-all(bf16[768,4,96]{0,2,1:T(8,128)(2,1)S(1)} %bitcast.34), channel_id=1, replica_groups=mesh['row'=16,'col'=8,'fiber'=4] {'fiber'}, dimensions={1} | all-to-all | bytes 1179648 | tf_op jit(solution)/shard_map/all_to_all | solution.py:47
  39.4 0.0 all-gather.3.cloned.1.call-update
  39.4 0.0 all-gather.5.cloned.1.call-start
  39.4 0.3 copy.28
  39.7 0.1 copy.29
  39.8 22.0 %all_to_all.22 = bf16[2,4,96,384]{3,2,0,1:T(8,128)(2,1)S(1)} all-to-all(bf16[2,4,96,384]{3,2,0,1:T(8,128)(2,1)S(1)} %copy.29), channel_id=1, replica_groups=mesh['row'=16,'col'=8,'fiber'=4] {'fiber'}, dimensions={1} | all-to-all | bytes 1179648 | tf_op jit(solution)/shard_map/all_to_all | solution.py:48
  61.9 0.5 copy.30
  62.3 0.9 copy.40
  63.2 0.0 all-gather.5.cloned.1.call-update
  63.2 34.8 %all-gather.3.cloned.1.call-done = bf16[768,3072]{0,1:T(8,128)(2,1)} async-done(((bf16[768,384]{0,1:T(8,128)(2,1)}), bf16[768,3072]{0,1:T(8,128)(2,1)}) %all-gather.3.cloned.1.call-update) | async-done | bytes 4718608 | tf_op jit(solution)/shard_map/all_gather | solution.py:54
  98.0 118.6 %all-gather.5.cloned.1.call-done = bf16[3072,1536]{1,0:T(8,128)(2,1)} async-done(((bf16[192,1536]{1,0:T(8,128)(2,1)}), bf16[3072,1536]{1,0:T(8,128)(2,1)}) %all-gather.5.cloned.1.call-update) | async-done | bytes 9437200 | tf_op jit(solution)/shard_map/all_gather | solution.py:57
  216.6 11.6 %convolution_convert_fusion = bf16[768,1536]{1,0:T(8,128)(2,1)S(1)} fusion(bf16[768,3072]{0,1:T(8,128)(2,1)} %all-gather.3.cloned.1.call-done, bf16[3072,1536]{1,0:T(8,128)(2,1)} %all-gather.5.cloned.1.call-done), kind=kOutput, calls=%fused_computation.1 | convolution fusion | flops 7248936960 | bytes 16515072 | tf_op jit(solution)/shard_map/dot_general | solution.py:55
  228.2 0.2 copy.44
  228.5 61.1 %all_to_all.23 = bf16[4,768,384]{2,1,0:T(8,128)(2,1)S(1)} all-to-all(bf16[4,768,384]{2,1,0:T(8,128)(2,1)S(1)} %bitcast.31), channel_id=1, replica_groups=mesh['row'=16,'col'=8,'fiber'=4] {'fiber'}, dimensions={0} | all-to-all | bytes 4718592 | tf_op jit(solution)/shard_map/all_to_all | solution.py:15
  289.6 0.0 copy-start
  289.6 0.4 convert_reduce_fusion
  289.9 0.1 multiply_reduce_fusion
  290.1 0.6 broadcast_in_dim.8
  290.7 4.1 %all-to-all-start.3 = ((f32[16,1,384]{2,1,0:T(1,128)}), f32[16,1,384]{2,1,0:T(1,128)}, u32[]{:S(2)}, u32[]{:S(2)}) async-start(f32[16,1,384]{2,1,0:T(1,128)} %broadcast_in_dim.8), calls=%async_computation.3 | async-start | bytes 49152 | tf_op jit(solution)/shard_map/all_to_all | solution.py:21
  294.8 0.0 copy-done
  294.9 0.2 broadcast_in_dim.6
  295.0 0.3 copy.45
  295.3 0.4 copy.33
  295.7 7.3 %all-to-all-done.3 = f32[16,1,384]{2,1,0:T(1,128)} async-done(((f32[16,1,384]{2,1,0:T(1,128)}), f32[16,1,384]{2,1,0:T(1,128)}, u32[]{:S(2)}, u32[]{:S(2)}) %all-to-all-start.3) | async-done | bytes 24608 | tf_op jit(solution)/shard_map/all_to_all | solution.py:21
  302.9 0.8 reduce_sum.29
  303.7 1.1 multiply_divide_fusion
  (2 shorter events, 0.0 us)
Async XLA Ops:
  6.5 91.5 %all-gather.3.cloned.1.call-start = ((), (), s32[]{:S(2)}) async-start(), calls=%async_computation.4 | async-start | bytes 5308416 | tf_op jit(solution)/shard_map/all_gather | solution.py:54
  39.4 177.2 %all-gather.5.cloned.1.call-start = ((), (), s32[]{:S(2)}) async-start(), calls=%async_computation.5 | async-start | bytes 10027008 | tf_op jit(solution)/shard_map/all_gather | solution.py:57
  289.6 5.3 %copy-start = (s32[6,3]{0,1:T(4,128)S(1)}, s32[6,3]{0,1:T(4,128)}, u32[]{:S(2)}) copy-start(s32[6,3]{0,1:T(4,128)} %param.5) | copy-start | bytes 220
  290.7 12.2 %all-to-all-start.3 = ((f32[16,1,384]{2,1,0:T(1,128)}), f32[16,1,384]{2,1,0:T(1,128)}, u32[]{:S(2)}, u32[]{:S(2)}) async-start(f32[16,1,384]{2,1,0:T(1,128)} %broadcast_in_dim.8), calls=%async_computation.3 | async-start | bytes 49152 | tf_op jit(solution)/shard_map/all_to_all | solution.py:21
Sparse Core Ops, SparseCore 0:
  39.5 58.4 all-gather.2
  100.1 116.4 all-gather.4
where the time goes:
time: 312 us
  waiting for transfers between devices  161 us (52%)
  blocking collectives  113 us (36%)
  between operations  13.5 us (4%)
  matrix products  11.6 us (4%)
  local copies, waits for them, and re-layouts  5.17 us (2%)
  starting transfers between devices  4.18 us (1%)
  other arithmetic  3.47 us (1%)
    all_gather x1, waiting for transfers between devices, local(): lax.all_gather(right_local, 'row', axis=0, tiled=True)  119 us
    all_to_all x1, blocking collectives, sum_at_owner(): lax.all_to_all(parts, axis, split_axis=0, concat_axis=0, tiled=True)  61.1 us
    all_gather x1, waiting for transfers between devices, local(): left_all = lax.all_gather(left_local, 'col', axis=1, tiled=True)  34.8 us
    all_to_all x1, blocking collectives, local(): lax.all_to_all(left_stack, 'fiber', split_axis=1, concat_axis=1, tiled=True)  30 us
    all_to_all x1, blocking collectives, local(): lax.all_to_all(right_stack, 'fiber', split_axis=1, concat_axis=1, tiled=T...  22 us
    dot_general x1, matrix products, local(): jnp.dot(left_all, lax.all_gather(right_local, 'row', axis=0, tiled=True),...  11.6 us
    all_to_all x1, waiting for transfers between devices, sent_to_all(): return lax.all_to_all(copies, axis, split_axis=0, concat_axis=0, tiled=True)  7.26 us
  transfers between devices with their start and end apart: 3, of which 3 were waited for; matrix products, arithmetic and copies ran while one was open for 1% of the time, Pallas kernels for 0%

commit v1 on v0

--- a/solution.py
+++ b/solution.py
@@ -51,7 +51,21 @@
     right_local = jnp.transpose(right_recv, (0, 2, 1, 3)).reshape(
         unit_count * sub_width, n_fib * unit_width
     )
-    left_all = lax.all_gather(left_local, "col", axis=1, tiled=True)
+    ways, here, turn = (lax.axis_size("col"), lax.axis_index("col"), left_local.shape[1])
+    shape = [n * ways if d == 1 else n for d, n in enumerate(left_local.shape)]
+    full = lax.dynamic_update_slice_in_dim(
+        jnp.zeros(shape, left_local.dtype), left_local, here * turn, axis=1
+    )
+    going_up = going_down = left_local
+    for far in range(1, ways // 2 + 1):
+        going_up = lax.ppermute(going_up, "col", [(d, (d + 1) % ways) for d in range(ways)])
+        full = lax.dynamic_update_slice_in_dim(full, going_up, (here - far) % ways * turn, axis=1)
+        if 2 * far < ways:
+            going_down = lax.ppermute(going_down, "col", [(d, (d - 1) % ways) for d in range(ways)])
+            full = lax.dynamic_update_slice_in_dim(
+                full, going_down, (here + far) % ways * turn, axis=1
+            )
+    left_all = full
     partial_product = jnp.dot(
         left_all,
         lax.all_gather(right_local, "row", axis=0, tiled=True),

time: 312 us -> 255 us (0.82)
  the two profiles are of different devices: /device:TPU:8 before, /device:TPU:56 now
where the time goes in v1:
time: 255 us; the launch traced here: 254 us
  blocking collectives  96.5 us (38%)
  waiting for transfers between devices  76 us (30%)
  starting transfers between devices  38.1 us (15%)
  local copies, waits for them, and re-layouts  14.7 us (6%)
  between operations  13.7 us (5%)
  matrix products  11.6 us (5%)
  other arithmetic  3.47 us (1%)
    all_to_all x1, blocking collectives, sum_at_owner(): lax.all_to_all(parts, axis, split_axis=0, concat_axis=0, tiled=True)  49.2 us
    all_gather x1, waiting for transfers between devices, local(): lax.all_gather(right_local, 'row', axis=0, tiled=True)  42.8 us
    all_to_all x1, blocking collectives, local(): lax.all_to_all(right_stack, 'fiber', split_axis=1, concat_axis=1, tiled=T...  29.9 us
    ppermute x4, waiting for transfers between devices, local(): lax.ppermute(going_up, 'col', [(d, (d + 1) % ways) for d in range(ways)])  25.9 us
    all_to_all x1, blocking collectives, local(): lax.all_to_all(left_stack, 'fiber', split_axis=1, concat_axis=1, tiled=True)  17.4 us
    ppermute x4, starting transfers between devices, local(): lax.ppermute(going_up, 'col', [(d, (d + 1) % ways) for d in range(ways)])  15.8 us
    all_to_all x1, starting transfers between devices, sent_to_all(): return lax.all_to_all(copies, axis, split_axis=0, concat_axis=0, tiled=True)  14.2 us
    dot_general x1, matrix products, local(): jnp.dot(left_all, lax.all_gather(right_local, 'row', axis=0, tiled=True),...  11.6 us
  transfers between devices with their start and end apart: 9, of which 6 were waited for; matrix products, arithmetic and copies ran while one was open for 4% of the time, Pallas kernels for 0%

profile of v1, /device:TPU:56, one launch (start us, length us, event | category | flops | bytes accessed | tf_op | source)
XLA Modules:
  0.0 254.1 jit_solution(12724763408935176923)
XLA Ops:
  6.5 0.7 convert_element_type.16
  7.2 1.6 copy.27
  8.9 0.2 broadcast_in_dim.10
  9.0 0.4 fusion
  9.4 0.3 copy.28
  9.7 0.1 copy.29
  9.8 29.9 %all_to_all.21 = bf16[2,4,96,384]{3,2,0,1:T(8,128)(2,1)S(1)} all-to-all(bf16[2,4,96,384]{3,2,0,1:T(8,128)(2,1)S(1)} %copy.29), channel_id=1, replica_groups=mesh['row'=16,'col'=8,'fiber'=4] {'fiber'}, dimensions={1} | all-to-all | bytes 1179648 | tf_op jit(solution)/shard_map/all_to_all | solution.py:48
  39.6 0.5 copy.30
  40.1 0.9 copy.40
  41.0 0.0 all-gather.2.cloned.1.call-update
  41.0 17.4 %all_to_all.22 = bf16[768,4,96]{0,2,1:T(8,128)(2,1)S(1)} all-to-all(bf16[768,4,96]{0,2,1:T(8,128)(2,1)S(1)} %bitcast.34), channel_id=1, replica_groups=mesh['row'=16,'col'=8,'fiber'=4] {'fiber'}, dimensions={1} | all-to-all | bytes 1179648 | tf_op jit(solution)/shard_map/all_to_all | solution.py:47
  58.4 2.1 collective-permute-start
  60.5 3.8 %collective-permute-start.1 = (bf16[768,384]{0,1:T(8,128)(2,1)S(1)}, bf16[768,384]{0,1:T(8,128)(2,1)S(1)}, u32[]{:S(2)}, u32[]{:S(2)}) collective-permute-start(bf16[768,384]{0,1:T(8,128)(2,1)S(1)} %bitcast.39), channel_id=1, source_target_pairs={{0,28},{4,0},{8,4},{12,8},{16,12},{20,16},{24,20},{28,24},{1,29},{... | collective-permute-start | bytes 1769480 | tf_op jit(solution)/shard_map/ppermute | solution.py:64
  64.3 9.6 %collective-permute-done = bf16[768,384]{0,1:T(8,128)(2,1)S(1)} collective-permute-done((bf16[768,384]{0,1:T(8,128)(2,1)S(1)}, bf16[768,384]{0,1:T(8,128)(2,1)S(1)}, u32[]{:S(2)}, u32[]{:S(2)}) %collective-permute-start) | collective-permute-done | bytes 589856 | tf_op jit(solution)/shard_map/ppermute | solution.py:61
  73.8 3.4 %collective-permute-start.2 = (bf16[768,384]{0,1:T(8,128)(2,1)S(1)}, bf16[768,384]{0,1:T(8,128)(2,1)S(1)}, u32[]{:S(2)}, u32[]{:S(2)}) collective-permute-start(bf16[768,384]{0,1:T(8,128)(2,1)S(1)} %collective-permute-done), channel_id=1, source_target_pairs={{0,4},{4,8},{8,12},{12,16},{16,20},{20,24},{24,28},{28,0},{1,5},{5... | collective-permute-start | bytes 1769480 | tf_op jit(solution)/shard_map/ppermute | solution.py:61
  77.3 0.0 collective-permute-done.1
  77.3 2.4 collective-permute-start.3
  79.7 8.8 %collective-permute-done.2 = bf16[768,384]{0,1:T(8,128)(2,1)S(1)} collective-permute-done((bf16[768,384]{0,1:T(8,128)(2,1)S(1)}, bf16[768,384]{0,1:T(8,128)(2,1)S(1)}, u32[]{:S(2)}, u32[]{:S(2)}) %collective-permute-start.2) | collective-permute-done | bytes 589856 | tf_op jit(solution)/shard_map/ppermute | solution.py:61
  88.5 4.7 %collective-permute-start.4 = (bf16[768,384]{0,1:T(8,128)(2,1)S(1)}, bf16[768,384]{0,1:T(8,128)(2,1)S(1)}, u32[]{:S(2)}, u32[]{:S(2)}) collective-permute-start(bf16[768,384]{0,1:T(8,128)(2,1)S(1)} %collective-permute-done.2), channel_id=1, source_target_pairs={{0,4},{4,8},{8,12},{12,16},{16,20},{20,24},{24,28},{28,0},{1,5},{5... | collective-permute-start | bytes 1769480 | tf_op jit(solution)/shard_map/ppermute | solution.py:61
  93.3 2.6 %broadcast_in_dim.9 = bf16[768,3072]{0,1:T(8,128)(2,1)} broadcast(bf16[]{:T(256)} %constant.54.clone.1), dimensions={} | broadcast | bytes 4718594 | tf_op jit(solution)/shard_map/broadcast_in_dim | solution.py:57
  95.9 0.8 constant_dynamic-update-slice_fusion.7
  96.7 0.0 collective-permute-done.3
  96.7 1.9 collective-permute-start.5
  98.7 0.9 constant_dynamic-update-slice_fusion.6
  99.6 3.2 %collective-permute-done.4 = bf16[768,384]{0,1:T(8,128)(2,1)S(1)} collective-permute-done((bf16[768,384]{0,1:T(8,128)(2,1)S(1)}, bf16[768,384]{0,1:T(8,128)(2,1)S(1)}, u32[]{:S(2)}, u32[]{:S(2)}) %collective-permute-start.4) | collective-permute-done | bytes 589856 | tf_op jit(solution)/shard_map/ppermute | solution.py:61
  102.7 5.6 %collective-permute-start.6 = (bf16[768,384]{0,1:T(8,128)(2,1)S(1)}, bf16[768,384]{0,1:T(8,128)(2,1)S(1)}, u32[]{:S(2)}, u32[]{:S(2)}) collective-permute-start(bf16[768,384]{0,1:T(8,128)(2,1)S(1)} %collective-permute-done.4), channel_id=1, source_target_pairs={{0,4},{4,8},{8,12},{12,16},{16,20},{20,24},{24,28},{28,0},{1,5},{5... | collective-permute-start | bytes 1769480 | tf_op jit(solution)/shard_map/ppermute | solution.py:61
  108.3 0.9 constant_dynamic-update-slice_fusion.5
  109.2 0.9 constant_dynamic-update-slice_fusion.4
  110.1 0.9 constant_dynamic-update-slice_fusion.3
  110.9 0.9 constant_dynamic-update-slice_fusion.2
  111.8 0.9 constant_dynamic-update-slice_fusion.1
  112.7 4.4 %collective-permute-done.6 = bf16[768,384]{0,1:T(8,128)(2,1)S(1)} collective-permute-done((bf16[768,384]{0,1:T(8,128)(2,1)S(1)}, bf16[768,384]{0,1:T(8,128)(2,1)S(1)}, u32[]{:S(2)}, u32[]{:S(2)}) %collective-permute-start.6) | collective-permute-done | bytes 589856 | tf_op jit(solution)/shard_map/ppermute | solution.py:61
  117.1 0.8 constant_dynamic-update-slice_fusion
  117.9 42.8 %all-gather.2.cloned.1.call-done = bf16[3072,1536]{1,0:T(8,128)(2,1)} async-done(((bf16[192,1536]{1,0:T(8,128)(2,1)}), bf16[3072,1536]{1,0:T(8,128)(2,1)}) %all-gather.2.cloned.1.call-update) | async-done | bytes 9437200 | tf_op jit(solution)/shard_map/all_gather | solution.py:71
  160.7 11.6 %convolution_convert_fusion = bf16[768,1536]{1,0:T(8,128)(2,1)S(1)} fusion(bf16[768,3072]{0,1:T(8,128)(2,1)} %constant_dynamic-update-slice_fusion, bf16[3072,1536]{1,0:T(8,128)(2,1)} %all-gather.2.cloned.1.call-done), kind=kOutput, calls=%fused_computation.1 | convolution fusion | flops 7248936960 | bytes 16515072 | tf_op jit(solution)/shard_map/dot_general | solution.py:69
  172.3 0.2 copy.44
  172.6 0.0 copy-start
  172.6 49.2 %all_to_all.23 = bf16[4,768,384]{2,1,0:T(8,128)(2,1)S(1)} all-to-all(bf16[4,768,384]{2,1,0:T(8,128)(2,1)S(1)} %bitcast.31), channel_id=1, replica_groups=mesh['row'=16,'col'=8,'fiber'=4] {'fiber'}, dimensions={0} | all-to-all | bytes 4718592 | tf_op jit(solution)/shard_map/all_to_all | solution.py:15
  221.8 0.4 convert_reduce_fusion
  222.2 0.1 multiply_reduce_fusion
  222.3 0.6 broadcast_in_dim.22
  222.9 14.2 %all-to-all-start.3 = ((f32[16,1,384]{2,1,0:T(1,128)}), f32[16,1,384]{2,1,0:T(1,128)}, u32[]{:S(2)}, u32[]{:S(2)}) async-start(f32[16,1,384]{2,1,0:T(1,128)} %broadcast_in_dim.22), calls=%async_computation.3 | async-start | bytes 49152 | tf_op jit(solution)/shard_map/all_to_all | solution.py:21
  237.2 0.2 broadcast_in_dim.8
  237.3 0.3 copy.45
  237.6 0.4 copy.33
  238.0 7.3 %all-to-all-done.3 = f32[16,1,384]{2,1,0:T(1,128)} async-done(((f32[16,1,384]{2,1,0:T(1,128)}), f32[16,1,384]{2,1,0:T(1,128)}, u32[]{:S(2)}, u32[]{:S(2)}) %all-to-all-start.3) | async-done | bytes 24608 | tf_op jit(solution)/shard_map/all_to_all | solution.py:21
  245.3 0.8 reduce_sum.29
  246.1 1.1 multiply_divide_fusion
  (5 shorter events, 0.0 us)
Async XLA Ops:
  6.5 154.2 %all-gather.2.cloned.1.call-start = ((), (), s32[]{:S(2)}) async-start(), calls=%async_computation.4 | async-start | bytes 10027008 | tf_op jit(solution)/shard_map/all_gather | solution.py:71
  58.4 15.4 %collective-permute-start = (bf16[768,384]{0,1:T(8,128)(2,1)S(1)}, bf16[768,384]{0,1:T(8,128)(2,1)S(1)}, u32[]{:S(2)}, u32[]{:S(2)}) collective-permute-start(bf16[768,384]{0,1:T(8,128)(2,1)S(1)} %bitcast.38), channel_id=1, source_target_pairs={{0,4},{4,8},{8,12},{12,16},{16,20},{20,24},{24,28},{28,0},{1,5},{5... | collective-permute-start | bytes 1769480 | tf_op jit(solution)/shard_map/ppermute | solution.py:61
  60.5 16.8 %collective-permute-start.1 = (bf16[768,384]{0,1:T(8,128)(2,1)S(1)}, bf16[768,384]{0,1:T(8,128)(2,1)S(1)}, u32[]{:S(2)}, u32[]{:S(2)}) collective-permute-start(bf16[768,384]{0,1:T(8,128)(2,1)S(1)} %bitcast.39), channel_id=1, source_target_pairs={{0,28},{4,0},{8,4},{12,8},{16,12},{20,16},{24,20},{28,24},{1,29},{... | collective-permute-start | bytes 1769480 | tf_op jit(solution)/shard_map/ppermute | solution.py:64
  73.8 14.6 %collective-permute-start.2 = (bf16[768,384]{0,1:T(8,128)(2,1)S(1)}, bf16[768,384]{0,1:T(8,128)(2,1)S(1)}, u32[]{:S(2)}, u32[]{:S(2)}) collective-permute-start(bf16[768,384]{0,1:T(8,128)(2,1)S(1)} %collective-permute-done), channel_id=1, source_target_pairs={{0,4},{4,8},{8,12},{12,16},{16,20},{20,24},{24,28},{28,0},{1,5},{5... | collective-permute-start | bytes 1769480 | tf_op jit(solution)/shard_map/ppermute | solution.py:61
  77.3 19.5 %collective-permute-start.3 = (bf16[768,384]{0,1:T(8,128)(2,1)S(1)}, bf16[768,384]{0,1:T(8,128)(2,1)S(1)}, u32[]{:S(2)}, u32[]{:S(2)}) collective-permute-start(bf16[768,384]{0,1:T(8,128)(2,1)S(1)} %collective-permute-done.1), channel_id=1, source_target_pairs={{0,28},{4,0},{8,4},{12,8},{16,12},{20,16},{24,20},{28,24},{1,29},{... | collective-permute-start | bytes 1769480 | tf_op jit(solution)/shard_map/ppermute | solution.py:64
  88.5 14.3 %collective-permute-start.4 = (bf16[768,384]{0,1:T(8,128)(2,1)S(1)}, bf16[768,384]{0,1:T(8,128)(2,1)S(1)}, u32[]{:S(2)}, u32[]{:S(2)}) collective-permute-start(bf16[768,384]{0,1:T(8,128)(2,1)S(1)} %collective-permute-done.2), channel_id=1, source_target_pairs={{0,4},{4,8},{8,12},{12,16},{16,20},{20,24},{24,28},{28,0},{1,5},{5... | collective-permute-start | bytes 1769480 | tf_op jit(solution)/shard_map/ppermute | solution.py:61
  96.7 15.1 %collective-permute-start.5 = (bf16[768,384]{0,1:T(8,128)(2,1)S(1)}, bf16[768,384]{0,1:T(8,128)(2,1)S(1)}, u32[]{:S(2)}, u32[]{:S(2)}) collective-permute-start(bf16[768,384]{0,1:T(8,128)(2,1)S(1)} %collective-permute-done.3), channel_id=1, source_target_pairs={{0,28},{4,0},{8,4},{12,8},{16,12},{20,16},{24,20},{28,24},{1,29},{... | collective-permute-start | bytes 1769480 | tf_op jit(solution)/shard_map/ppermute | solution.py:64
  102.7 14.3 %collective-permute-start.6 = (bf16[768,384]{0,1:T(8,128)(2,1)S(1)}, bf16[768,384]{0,1:T(8,128)(2,1)S(1)}, u32[]{:S(2)}, u32[]{:S(2)}) collective-permute-start(bf16[768,384]{0,1:T(8,128)(2,1)S(1)} %collective-permute-done.4), channel_id=1, source_target_pairs={{0,4},{4,8},{8,12},{12,16},{16,20},{20,24},{24,28},{28,0},{1,5},{5... | collective-permute-start | bytes 1769480 | tf_op jit(solution)/shard_map/ppermute | solution.py:61
  172.6 64.6 %copy-start = (s32[6,3]{0,1:T(4,128)S(1)}, s32[6,3]{0,1:T(4,128)}, u32[]{:S(2)}) copy-start(s32[6,3]{0,1:T(4,128)} %param.5) | copy-start | bytes 220
  222.9 22.4 %all-to-all-start.3 = ((f32[16,1,384]{2,1,0:T(1,128)}), f32[16,1,384]{2,1,0:T(1,128)}, u32[]{:S(2)}, u32[]{:S(2)}) async-start(f32[16,1,384]{2,1,0:T(1,128)} %broadcast_in_dim.22), calls=%async_computation.3 | async-start | bytes 49152 | tf_op jit(solution)/shard_map/all_to_all | solution.py:21
Sparse Core Ops, SparseCore 0:
  41.1 119.5 all-gather.1
